TPU v7x, 32 devices: a whole 2x2x4 slice. The times are simulated.
32 devices in a mesh: groups: 2 (over x), lon: 16 (over z, y, core).
Axes of the slice: x: 2, y: 2, z: 4, core: 2. Of those that a mesh axis runs over, the one named last changes fastest.
Arguments:
- latlon_fields: bfloat16 [32, 32, 2048], P('groups', 'lon'), parts along dimension 0, may hold values from -6 to 6
- remap_table: int32 [2, 32, 2048], P(None, None, 'lon'), may hold values from 0 to 2047, as said below
- kernel_first: bfloat16 [3, 3, 64, 16], replicated, may hold values from -0.5 to 0.5
- kernel_second: bfloat16 [3, 3, 64, 64], replicated, may hold values from -0.25 to 0.25
- kernel_down: bfloat16 [3, 3, 128, 64], replicated, may hold values from -0.25 to 0.25
- kernel_coarse: bfloat16 [3, 3, 128, 128], replicated, may hold values from -0.1875 to 0.1875
- kernel_up: bfloat16 [3, 3, 64, 128], replicated, may hold values from -0.375 to 0.375
- kernel_merge: bfloat16 [3, 3, 64, 128], replicated, may hold values from -0.1875 to 0.1875
- projection: bfloat16 [8, 64], replicated, may hold values from -0.75 to 0.75
Outputs:
- forecast: float32 [16, 32, 2048], P('groups', None, 'lon'), parts along dimension 0
There are 2 independent parts, one for each index of `groups`. A program takes and returns all parts, laid end to end along the dimension named above; an argument that names none is the same for every part. Nothing has to cross between parts.
Inputs may be any that keep to these rules, and one draw needn't show every extreme that they name: remap_table[0] is a lat-lon row below 32; remap_table[1] is a lat-lon column, and for a grid cell in column w it lies in the same block of 128 columns as w, that is between (w // 128) * 128 and (w // 128) * 128 + 127.
All inputs are finite; a program needn't handle non-finite values.
Results may differ from a plain program's by a relative error of at most 0.00084.
Values may be sent and summed in bfloat16 or wider, within the bound.
A program may use at most 128 MiB of HBM per device.

v0:
```python
import functools

import jax
import jax.numpy as jnp
from jax import lax
from jax.experimental import pallas as pl
from jax.experimental.pallas import tpu as pltpu
from jax.sharding import PartitionSpec as P

MESH = pl.DeviceIdType.MESH
F32 = jnp.float32
BF16 = jnp.bfloat16
HALO = 8
POLE = 8
OFFSETS = (0, 1, 2, -1)
NT = (((1,), (1,)), ((), ()))


def dot_nt(a, b):
    return lax.dot_general(a, b, NT, preferred_element_type=F32)


def silu(x):
    half = 0.5 * x
    return half * jnp.tanh(half) + half


def exchange_kernel(n, lat_ref, tab_ref, own_ref, left_ref, right_ref, anti_ref, recv, send_sem, recv_sem, own_sem, hsend, hrecv):
    me = lax.axis_index("lon")
    group = lax.axis_index("groups")
    cols = recv.shape[2]
    height = tab_ref.shape[1]
    channels = own_ref.shape[1]
    sub_rows = lat_ref.shape[0] // channels
    barrier = pltpu.get_barrier_semaphore()

    def greet(d, carry):
        pl.semaphore_signal(barrier, inc=1, device_id=(group, lax.rem(me + d, n)), device_id_type=MESH)
        return carry

    lax.fori_loop(1, n, greet, 0)
    mine = pltpu.make_async_copy(lat_ref.at[:, pl.ds(pl.multiple_of(me * cols, cols), cols)], recv.at[me], own_sem)
    mine.start()
    pl.semaphore_wait(barrier, n - 1)

    def block_copy(d, slot):
        target = lax.rem(me + d, n)
        return pltpu.make_async_remote_copy(
            src_ref=lat_ref.at[:, pl.ds(pl.multiple_of(target * cols, cols), cols)],
            dst_ref=recv.at[slot],
            send_sem=send_sem.at[d - 1],
            recv_sem=recv_sem.at[d - 1],
            device_id=(group, target),
            device_id_type=MESH,
        )

    def send(d, carry):
        block_copy(d, me).start()
        return carry

    lax.fori_loop(1, n, send, 0)

    p = lax.broadcasted_iota(jnp.int32, (cols, cols), 1)
    w = lax.broadcasted_iota(jnp.int32, (cols, cols), 0)
    half = cols // 2
    perm = (w == jnp.where(p < half, 2 * p, 2 * p - cols + 1)).astype(F32).astype(BF16)
    rows_at = jnp.dot(tab_ref[0].astype(F32).astype(BF16), perm, preferred_element_type=F32).astype(jnp.int32)
    cols_at = jnp.dot((tab_ref[1] - me * cols).astype(F32).astype(BF16), perm, preferred_element_type=F32).astype(jnp.int32)

    mine.wait()

    def receive(d, carry):
        block_copy(d, lax.rem(me - d + n, n)).wait_recv()
        return carry

    lax.fori_loop(1, n, receive, 0)

    at_col = lax.broadcasted_iota(jnp.int32, (cols, cols), 0)
    source = recv[...].reshape(n * lat_ref.shape[0], cols)
    chunk = 512
    total = source.shape[0]
    for h in range(0, height, 2):
        hot = jnp.concatenate(
            [(at_col == cols_at[h + q : h + q + 1]).astype(F32).astype(BF16) for q in range(2)], axis=1
        )
        row_sel = jnp.concatenate([rows_at[h : h + 1], rows_at[h + 1 : h + 2]], axis=1)
        picked = jnp.zeros((channels, 2 * cols), F32)
        for c0 in range(0, total, chunk):
            size = min(chunk, total - c0)
            got = jnp.dot(source[c0 : c0 + size], hot, preferred_element_type=F32)
            for r in range(size // channels):
                picked = jnp.where(row_sel == c0 // channels + r, got[r * channels : (r + 1) * channels], picked)
        for q in range(2):
            own_ref[h + q] = picked[:, q * cols : (q + 1) * cols].astype(BF16)

    def halo(k, src, dst, shift):
        return pltpu.make_async_remote_copy(
            src_ref=src, dst_ref=dst, send_sem=hsend.at[k], recv_sem=hrecv.at[k],
            device_id=(group, lax.rem(me + shift + 2 * n, n)), device_id_type=MESH)

    top = own_ref.at[pl.ds(0, POLE)]
    copies = [
        halo(0, own_ref, left_ref, 1),
        halo(1, own_ref, right_ref, -1),
        halo(2, top, anti_ref.at[0], n // 2),
        halo(3, top, anti_ref.at[1], n // 2 + 1),
        halo(4, top, anti_ref.at[2], n // 2 - 1),
    ]
    for c in copies:
        c.start()

    def sent(d, carry):
        block_copy(d, me).wait_send()
        return carry

    lax.fori_loop(1, n, sent, 0)
    for c in copies:
        c.wait()


def unet_kernel(own_ref, left_ref, right_ref, anti_ref, k1, k2, kd, kc, ku, km, kp, out_ref,
                xf, x1, x2, x3, xc, xu, w1, w2, wd, wc, wu, wma, wmb, wp):
    height, channels, cols = own_ref.shape
    half = cols // 2
    J = half + 2 * HALO
    C = k1.shape[2]
    C2 = kd.shape[2]
    COUT = kp.shape[0]
    pairs = height // 2
    AB = pairs + 1

    for w in (w1, w2, wd, wc, wu, wma, wmb, wp):
        w[...] = jnp.zeros_like(w)

    def fill(w, kernel, cin, first_in):
        for q in range(2):
            for p in range(2):
                for a in range(4):
                    for l, off in enumerate(OFFSETS):
                        kr, kcol = a - q, off - p + 1
                        if 0 <= kr < 3 and 0 <= kcol < 3:
                            at = (q * 2 + p) * C
                            lane = a * 4 * cin + l * cin
                            w[at : at + C, lane : lane + cin] = kernel[kr, kcol][:, first_in : first_in + cin]

    fill(w1, k1, channels, 0)
    fill(w2, k2, C, 0)
    fill(wma, km, C, 0)
    fill(wmb, km, C, C)
    for a in range(3):
        for l, kcol in ((0, 1), (1, 2), (3, 0)):
            wd[:, a * 4 * C + l * C : a * 4 * C + (l + 1) * C] = kd[a, kcol]
        for s, kcol in enumerate((1, 2, 0)):
            wc[:, (a * 3 + s) * C2 : (a * 3 + s + 1) * C2] = kc[a, kcol]
    for q, rows in ((0, ((0, 1),)), (1, ((0, 0), (1, 2)))):
        for p, columns in ((0, ((0, 1),)), (1, ((0, 0), (1, 2)))):
            at = (q * 2 + p) * C
            for ri, kr in rows:
                for ci, kcol in columns:
                    lane = (ri * 2 + ci) * C2
                    wu[at : at + C, lane : lane + C2] = ku[kr, kcol]
    for g in range(4):
        wp[g * COUT : (g + 1) * COUT, g * C : (g + 1) * C] = kp[...].astype(F32)

    def spread(g, l, r):
        lane = lax.broadcasted_iota(jnp.int32, g.shape, 1)
        even = jnp.where(lane < half, g, jnp.where(lane < half + HALO, pltpu.roll(r, half, 1), pltpu.roll(l, 2 * HALO, 1)))
        odd = jnp.where(lane < half, pltpu.roll(g, half, 1),
                        jnp.where(lane < half + HALO, r, pltpu.roll(l, half + 2 * HALO, 1)))
        after = jnp.where(lane == J - 1, pltpu.roll(even, J - 1, 1), pltpu.roll(even, cols - 1, 1))
        before = jnp.where(lane == 0, pltpu.roll(odd, cols - J + 1, 1), pltpu.roll(odd, 1, 1))
        return jnp.concatenate([even, odd, after, before], axis=0)

    tap = 4 * channels

    def put(slot, value):
        i, a = slot // 2, slot % 2
        if i < xf.shape[0]:
            xf[i, :, a * tap : (a + 1) * tap] = value
        if i > 0:
            xf[i - 1, :, (a + 2) * tap : (a + 3) * tap] = value

    for h in range(height):
        value = spread(own_ref[h].astype(F32), left_ref[h].astype(F32), right_ref[h].astype(F32)).T[:J].astype(BF16)
        put(h + 1, value)
        if h == 0:
            put(height + 2, value)
    for h in range(POLE - 1):
        value = spread(anti_ref[0, h].astype(F32), anti_ref[1, h].astype(F32), anti_ref[2, h].astype(F32)).T[:J].astype(BF16)
        put(height + 3 + h, value)
        if h == 0:
            put(0, value)
    put(height + 1, jnp.zeros((J, tap), BF16))

    def neighbours(v):
        count = v.shape[0]
        v = v.reshape(count // J, J, v.shape[1])
        lane = lax.broadcasted_iota(jnp.int32, v.shape, 2)
        other = jnp.where(lane < C, pltpu.roll(v, J - 1, 1), pltpu.roll(v, 1, 1))
        return jnp.concatenate([v, other], axis=2).astype(BF16)

    def store_pair(x, i0, count, s):
        x[pl.ds(i0, count), 1] = neighbours(s[:, : 2 * C])
        x[pl.ds(i0 + 1, count), 0] = neighbours(s[:, 2 * C :])

    def wrap(x):
        x[0, 0] = x[AB, 1]
        x[AB, 0] = x[0, 1]
        x[AB - 1, 1] = jnp.zeros(x.shape[2:], BF16)

    def taps(x, i0, count, a, width):
        v = x[pl.ds(i0 + a // 2, count), a % 2, 0:width]
        return v.reshape(count * width, v.shape[-1])

    def own_loop(steps, body):
        def run(t, carry):
            body(t)
            return carry
        lax.fori_loop(0, steps, run, 0)

    B = 4

    def first(i0, count):
        store_pair(x1, i0, count, silu(dot_nt(xf[pl.ds(i0, count)].reshape(count * J, 4 * tap), w1[...])))

    first(AB, 3)
    own_loop(pairs // B, lambda t: first(t * B, B))
    wrap(x1)

    def second(i0, count):
        acc = dot_nt(taps(x1, i0, count, 0, J), w2[:, : 4 * C])
        for a in range(1, 4):
            acc += dot_nt(taps(x1, i0, count, a, J), w2[:, a * 4 * C : (a + 1) * 4 * C])
        store_pair(x2, i0, count, silu(acc))

    second(AB, 2)
    own_loop(pairs // B, lambda t: second(t * B, B))
    wrap(x2)

    def shifts(v, both):
        v = v.reshape(v.shape[0] // J, J, v.shape[1])
        parts = [v, pltpu.roll(v, J - 1, 1)]
        if both:
            parts.append(pltpu.roll(v, 1, 1))
        return jnp.concatenate(parts, axis=2).astype(BF16)

    def down(i0, slot, count):
        acc = dot_nt(taps(x2, i0, count, 0, J), wd[:, : 4 * C])
        for a in range(1, 3):
            acc += dot_nt(taps(x2, i0, count, a, J), wd[:, a * 4 * C : (a + 1) * 4 * C])
        xc[pl.ds(slot, count)] = shifts(silu(acc), True)

    down(AB, pairs + 3, 2)
    own_loop(pairs // B, lambda t: down(t * B, t * B + 1, B))
    xc[0] = xc[pairs + 3]
    xc[pairs + 2] = xc[1]
    xc[pairs + 1] = jnp.zeros(xc.shape[1:], BF16)

    def coarse(i0, slot, count):
        acc = None
        for a in range(3):
            v = xc[pl.ds(i0 + a, count)].reshape(count * J, 3 * C2)
            part = dot_nt(v, wc[:, a * 3 * C2 : (a + 1) * 3 * C2])
            acc = part if acc is None else acc + part
        xu[pl.ds(slot, count)] = shifts(silu(acc), False)

    coarse(pairs + 2, pairs + 1, 1)
    own_loop(pairs // B, lambda t: coarse(t * B, t * B, B))
    xu[pairs] = jnp.zeros(xu.shape[1:], BF16)

    def up(i0, count):
        acc = dot_nt(xu[pl.ds(i0, count)].reshape(count * J, 2 * C2), wu[:, : 2 * C2])
        return silu(acc + dot_nt(xu[pl.ds(i0 + 1, count)].reshape(count * J, 2 * C2), wu[:, 2 * C2 :]))

    def up_own(t):
        store_pair(x3, t * B, B, up(t * B, B))

    own_loop(pairs // B, up_own)
    v = xu[pairs + 1]
    x3[0, 0] = neighbours(silu(dot_nt(v, wu[0 : 2 * C, : 2 * C2])))[0]
    x3[AB - 1, 1] = jnp.zeros(x3.shape[2:], BF16)

    p = lax.broadcasted_iota(jnp.int32, (cols, cols), 0)
    w = lax.broadcasted_iota(jnp.int32, (cols, cols), 1)
    unperm = (w == jnp.where(p < half, 2 * p, 2 * p - cols + 1)).astype(F32)
    wpb = wp[...].astype(BF16)

    for t in range(pairs // B):
        i0 = t * B
        acc = None
        for a in range(4):
            for x, w in ((x2, wma), (x3, wmb)):
                part = dot_nt(taps(x, i0, B, a, half), w[:, a * 4 * C : (a + 1) * 4 * C])
                acc = part if acc is None else acc + part
        merged = silu(acc).astype(BF16)
        update = dot_nt(wpb, merged)
        lines = []
        for b in range(B):
            u = update[:, b * half : (b + 1) * half]
            for q in range(2):
                line = jnp.concatenate([u[2 * q * COUT : (2 * q + 1) * COUT], u[(2 * q + 1) * COUT : (2 * q + 2) * COUT]], axis=1)
                lines.append(line + own_ref[2 * (i0 + b) + q].astype(F32)[:COUT])
        woven = jnp.dot(jnp.concatenate(lines, axis=0), unperm, precision=lax.Precision.HIGHEST, preferred_element_type=F32)
        for m in range(2 * B):
            out_ref[:, 2 * i0 + m, :] = woven[m * COUT : (m + 1) * COUT]


def shards(latlon, table, k1, k2, kd, kc, ku, km, kp):
    n = lax.axis_size("lon")
    channels, sub_rows, width = latlon.shape
    height, cols = table.shape[1], table.shape[2]
    lat = jnp.swapaxes(latlon, 0, 1).reshape(sub_rows * channels, width)
    vm = pl.BlockSpec(memory_space=pltpu.VMEM)
    field = jax.ShapeDtypeStruct((height, channels, cols), BF16)
    own, left, right, anti = pl.pallas_call(
        functools.partial(exchange_kernel, n),
        out_shape=(field, field, field, jax.ShapeDtypeStruct((3, POLE, channels, cols), BF16)),
        in_specs=[vm] * 2,
        out_specs=(vm,) * 4,
        scratch_shapes=[
            pltpu.VMEM((n, sub_rows * channels, cols), BF16),
            pltpu.SemaphoreType.DMA((n - 1,)),
            pltpu.SemaphoreType.DMA((n - 1,)),
            pltpu.SemaphoreType.DMA,
            pltpu.SemaphoreType.DMA((5,)),
            pltpu.SemaphoreType.DMA((5,)),
        ],
        compiler_params=pltpu.CompilerParams(collective_id=0, has_side_effects=True, vmem_limit_bytes=48 * 2**20),
        name="exchange",
    )(lat, table)
    C, C2, COUT = k1.shape[2], kd.shape[2], kp.shape[0]
    J = cols // 2 + 2 * HALO
    pairs = height // 2
    return pl.pallas_call(
        unet_kernel,
        out_shape=jax.ShapeDtypeStruct((COUT, height, cols), F32),
        in_specs=[vm] * 11,
        out_specs=vm,
        scratch_shapes=[
            pltpu.VMEM((pairs + 4, J, 16 * channels), BF16),
            pltpu.VMEM((pairs + 5, 2, J, 4 * C), BF16),
            pltpu.VMEM((pairs + 4, 2, J, 4 * C), BF16),
            pltpu.VMEM((pairs + 1, 2, J, 4 * C), BF16),
            pltpu.VMEM((pairs + 5, J, 3 * C2), BF16),
            pltpu.VMEM((pairs + 2, J, 2 * C2), BF16),
            pltpu.VMEM((4 * C, 16 * channels), BF16),
            pltpu.VMEM((4 * C, 16 * C), BF16),
            pltpu.VMEM((C2, 12 * C), BF16),
            pltpu.VMEM((C2, 9 * C2), BF16),
            pltpu.VMEM((4 * C, 4 * C2), BF16),
            pltpu.VMEM((4 * C, 16 * C), BF16),
            pltpu.VMEM((4 * C, 16 * C), BF16),
            pltpu.VMEM((4 * COUT, 4 * C), F32),
        ],
        compiler_params=pltpu.CompilerParams(vmem_limit_bytes=48 * 2**20),
        name="unet",
    )(own, left, right, anti, k1, k2, kd, kc, ku, km, kp)


def solution(mesh):
    return jax.shard_map(
        shards,
        mesh=mesh,
        in_specs=(P("groups", "lon", None), P(None, None, "lon")) + (P(),) * 7,
        out_specs=P("groups", None, "lon"),
        check_vma=False,
    )
```

profile of v0, /device:TPU:1, one launch (start us, length us, event | category | flops | bytes accessed | tf_op | source)
XLA Modules:
  0.0 42.0 jit_solution(15854512791166769824)
XLA Ops:
  0.0 0.0 copy-start.4
  0.0 0.0 copy-start.6
  0.0 1.0 %copy.10 = bf16[2,16,2048]{2,1,0:T(8,128)(2,1)S(1)} copy(bf16[2,16,2048]{2,0,1:T(2,128)(2,1)} %bitcast.3) | data formatting | bytes 262144 | tf_op jit(solution)/shard_map/transpose | solution.py:312
  1.0 0.0 copy-done.4
  1.0 0.0 copy-start.7
  1.0 0.0 copy-start.3
  1.0 19.9 %exchange.1 = (bf16[32,16,128]{2,1,0:T(8,128)(2,1)S(1)}, bf16[32,16,128]{2,1,0:T(8,128)(2,1)S(1)}, bf16[32,16,128]{2,1,0:T(8,128)(2,1)S(1)}, bf16[3,8,16,128]{3,2,1,0:T(8,128)(2,1)S(1)}) custom-call(bf16[32,2048]{1,0:T(8,128)(2,1)S(1)} %bitcast.2, s32[2,32,128]{2,1,0:T(8,128)S(1)} %copy-done.4), custom_call_target="tpu_custom_call" | custom-call | tf_op jit(solution)/shard_map/exchange/pallas_call | solution.py:315
  20.9 0.0 copy-done.6
  20.9 0.0 copy-start
  20.9 0.0 copy-start.2
  20.9 0.2 copy.12.kd
  21.2 0.0 copy-done.7
  21.2 0.0 copy-start.1
  21.2 0.0 copy-start.5
  21.2 0.1 copy.11.k1
  21.3 0.0 copy-done.3
  21.3 0.5 %copy-done = bf16[3,3,128,128]{3,2,1,0:T(8,128)(2,1)S(1)} copy-done((bf16[3,3,128,128]{3,2,1,0:T(8,128)(2,1)S(1)}, bf16[3,3,128,128]{3,2,1,0:T(8,128)(2,1)}, u32[]{:S(2)}) %copy-start) | copy-done | bytes 294936
  21.9 0.0 copy-done.2
  21.9 0.2 copy-done.1
  22.1 0.0 copy-done.5
  22.1 19.8 %unet.1 = f32[8,32,128]{2,1,0:T(8,128)} custom-call(bf16[32,16,128]{2,1,0:T(8,128)(2,1)S(1)} %get-tuple-element.9.own_ref, bf16[32,16,128]{2,1,0:T(8,128)(2,1)S(1)} %get-tuple-element.10.left_ref, bf16[32,16,128]{2,1,0:T(8,128)(2,1)S(1)} %get-tuple-element.11.right_ref, bf16[3,8,16,128]{3,2,1,0:T(8,128)(2,1)S(1)} %get-tuple-element.12.anti_ref, ...), custom_call_target="tpu_custom_call" | custom-call | tf_op jit(solution)/shard_map/unet/pallas_call | solution.py:334
Async XLA Ops:
  0.0 1.0 %copy-start.4 = (s32[2,32,128]{2,1,0:T(8,128)S(1)}, s32[2,32,128]{2,1,0:T(8,128)}, u32[]{:S(2)}) copy-start(s32[2,32,128]{2,1,0:T(8,128)} %tab_ref.1) | copy-start | bytes 98308
  0.0 20.9 %copy-start.6 = (bf16[3,3,128,64]{2,3,1,0:T(8,128)(2,1)S(1)}, bf16[3,3,128,64]{2,3,1,0:T(8,128)(2,1)}, u32[]{:S(2)}) copy-start(bf16[3,3,128,64]{2,3,1,0:T(8,128)(2,1)} %param.13) | copy-start | bytes 442372
  1.0 20.2 %copy-start.7 = (bf16[3,3,64,16]{2,3,1,0:T(8,128)(2,1)S(1)}, bf16[3,3,64,16]{2,3,1,0:T(8,128)(2,1)}, u32[]{:S(2)}) copy-start(bf16[3,3,64,16]{2,3,1,0:T(8,128)(2,1)} %param.11) | copy-start | bytes 55300
  1.0 20.3 %copy-start.3 = (bf16[3,3,64,128]{3,2,1,0:T(8,128)(2,1)S(1)}, bf16[3,3,64,128]{3,2,1,0:T(8,128)(2,1)}, u32[]{:S(2)}) copy-start(bf16[3,3,64,128]{3,2,1,0:T(8,128)(2,1)} %km.1) | copy-start | bytes 442372
  20.9 1.0 %copy-start = (bf16[3,3,128,128]{3,2,1,0:T(8,128)(2,1)S(1)}, bf16[3,3,128,128]{3,2,1,0:T(8,128)(2,1)}, u32[]{:S(2)}) copy-start(bf16[3,3,128,128]{3,2,1,0:T(8,128)(2,1)} %kc.1) | copy-start | bytes 884740
  20.9 1.0 %copy-start.2 = (bf16[3,3,64,128]{3,2,1,0:T(8,128)(2,1)S(1)}, bf16[3,3,64,128]{3,2,1,0:T(8,128)(2,1)}, u32[]{:S(2)}) copy-start(bf16[3,3,64,128]{3,2,1,0:T(8,128)(2,1)} %ku.1) | copy-start | bytes 442372
  21.2 1.0 %copy-start.1 = (bf16[3,3,64,64]{3,2,1,0:T(8,128)(2,1)S(1)}, bf16[3,3,64,64]{3,2,1,0:T(8,128)(2,1)}, u32[]{:S(2)}) copy-start(bf16[3,3,64,64]{3,2,1,0:T(8,128)(2,1)} %k2.1) | copy-start | bytes 221188
  21.2 0.9 %copy-start.5 = (bf16[8,64]{1,0:T(8,128)(2,1)S(1)}, bf16[8,64]{1,0:T(8,128)(2,1)}, u32[]{:S(2)}) copy-start(bf16[8,64]{1,0:T(8,128)(2,1)} %kp.1) | copy-start | bytes 3076
where the time goes:
time: 42.1 us; the launch traced here: 42 us
  Pallas kernels  39.7 us (94%)
  local copies, waits for them, and re-layouts  2.17 us (5%)
    pallas_call x1, Pallas kernels, shards(): pl.pallas_call(functools.partial(exchange_kernel, n), out_shape=(field, f...  19.9 us
    pallas_call x1, Pallas kernels, shards(): pl.pallas_call(unet_kernel, out_shape=jax.ShapeDtypeStruct((COUT, height,...  19.8 us
    unnamed x18, local copies, waits for them, and re-layouts  1.19 us
    transpose x1, local copies, waits for them, and re-layouts, shards(): lat = jnp.swapaxes(latlon, 0, 1).reshape(sub_rows * channels, width)  0.98 us

commit v1 on v0

--- a/solution.py
+++ b/solution.py
@@ -11,7 +11,7 @@
 F32 = jnp.float32
 BF16 = jnp.bfloat16
 HALO = 8
-POLE = 8
+PER = 8
 OFFSETS = (0, 1, 2, -1)
 NT = (((1,), (1,)), ((), ()))
 
@@ -25,13 +25,14 @@
     return half * jnp.tanh(half) + half
 
 
-def exchange_kernel(n, lat_ref, tab_ref, own_ref, left_ref, right_ref, anti_ref, recv, send_sem, recv_sem, own_sem, hsend, hrecv):
+def exchange_kernel(n, lat_ref, tab_ref, own_ref, left_ref, right_ref, anti_ref, anti_left_ref, anti_right_ref,
+                    recv, edge, send_sem, recv_sem, own_sem, hsend, hrecv):
     me = lax.axis_index("lon")
     group = lax.axis_index("groups")
     cols = recv.shape[2]
     height = tab_ref.shape[1]
-    channels = own_ref.shape[1]
-    sub_rows = lat_ref.shape[0] // channels
+    per = height // own_ref.shape[0]
+    channels = own_ref.shape[2] // per
     barrier = pltpu.get_barrier_semaphore()
 
     def greet(d, carry):
@@ -60,12 +61,19 @@
 
     lax.fori_loop(1, n, send, 0)
 
-    p = lax.broadcasted_iota(jnp.int32, (cols, cols), 1)
-    w = lax.broadcasted_iota(jnp.int32, (cols, cols), 0)
+    p = lax.broadcasted_iota(jnp.int32, (cols, cols), 0)
+    w = lax.broadcasted_iota(jnp.int32, (cols, cols), 1)
     half = cols // 2
     perm = (w == jnp.where(p < half, 2 * p, 2 * p - cols + 1)).astype(F32).astype(BF16)
-    rows_at = jnp.dot(tab_ref[0].astype(F32).astype(BF16), perm, preferred_element_type=F32).astype(jnp.int32)
-    cols_at = jnp.dot((tab_ref[1] - me * cols).astype(F32).astype(BF16), perm, preferred_element_type=F32).astype(jnp.int32)
+    rows_at = dot_nt(perm, tab_ref[0].astype(F32).astype(BF16)).astype(jnp.int32)
+    cols_at = dot_nt(perm, (tab_ref[1] - me * cols).astype(F32).astype(BF16)).astype(jnp.int32)
+    wide = per * channels
+    lane = lax.broadcasted_iota(jnp.int32, (cols, wide), 1)
+    hots = [(cols_at[:, h : h + 1] == w).astype(F32).astype(BF16) for h in range(height)]
+    at_row = [jnp.broadcast_to(rows_at[:, h : h + 1], (cols, wide)) - lane // channels for h in range(height)]
+    fi = lax.broadcasted_iota(jnp.int32, (per * wide, wide), 0)
+    fo = lax.broadcasted_iota(jnp.int32, (per * wide, wide), 1)
+    fold = ((fi // wide == fo // channels) & (fi % channels == fo % channels)).astype(F32).astype(BF16)
 
     mine.wait()
 
@@ -75,36 +83,33 @@
 
     lax.fori_loop(1, n, receive, 0)
 
-    at_col = lax.broadcasted_iota(jnp.int32, (cols, cols), 0)
     source = recv[...].reshape(n * lat_ref.shape[0], cols)
-    chunk = 512
-    total = source.shape[0]
-    for h in range(0, height, 2):
-        hot = jnp.concatenate(
-            [(at_col == cols_at[h + q : h + q + 1]).astype(F32).astype(BF16) for q in range(2)], axis=1
-        )
-        row_sel = jnp.concatenate([rows_at[h : h + 1], rows_at[h + 1 : h + 2]], axis=1)
-        picked = jnp.zeros((channels, 2 * cols), F32)
-        for c0 in range(0, total, chunk):
-            size = min(chunk, total - c0)
-            got = jnp.dot(source[c0 : c0 + size], hot, preferred_element_type=F32)
-            for r in range(size // channels):
-                picked = jnp.where(row_sel == c0 // channels + r, got[r * channels : (r + 1) * channels], picked)
-        for q in range(2):
-            own_ref[h + q] = picked[:, q * cols : (q + 1) * cols].astype(BF16)
+    tiles = source.shape[0] // wide
+    for g in range(own_ref.shape[0]):
+        got = dot_nt(jnp.concatenate(hots[g * per : (g + 1) * per], axis=0), source)
+        picked = []
+        for q in range(per):
+            one = jnp.zeros((cols, wide), F32)
+            for t in range(tiles):
+                value = got[q * cols : (q + 1) * cols, t * wide : (t + 1) * wide]
+                one = jnp.where(at_row[g * per + q] == t * per, value, one)
+            picked.append(one.astype(BF16))
+        block = jnp.dot(jnp.concatenate(picked, axis=1), fold, preferred_element_type=F32)
+        own_ref[g] = block.astype(BF16)
+        edge[0, g] = jnp.concatenate([block[0:HALO], block[half : half + HALO]], axis=0).astype(BF16)
+        edge[1, g] = jnp.concatenate([block[half - HALO : half], block[cols - HALO : cols]], axis=0).astype(BF16)
 
     def halo(k, src, dst, shift):
         return pltpu.make_async_remote_copy(
             src_ref=src, dst_ref=dst, send_sem=hsend.at[k], recv_sem=hrecv.at[k],
             device_id=(group, lax.rem(me + shift + 2 * n, n)), device_id_type=MESH)
 
-    top = own_ref.at[pl.ds(0, POLE)]
     copies = [
-        halo(0, own_ref, left_ref, 1),
-        halo(1, own_ref, right_ref, -1),
-        halo(2, top, anti_ref.at[0], n // 2),
-        halo(3, top, anti_ref.at[1], n // 2 + 1),
-        halo(4, top, anti_ref.at[2], n // 2 - 1),
+        halo(0, own_ref.at[0], anti_ref, n // 2),
+        halo(1, edge.at[1], left_ref, 1),
+        halo(2, edge.at[0], right_ref, -1),
+        halo(3, edge.at[1, 0], anti_left_ref, n // 2 + 1),
+        halo(4, edge.at[0, 0], anti_right_ref, n // 2 - 1),
     ]
     for c in copies:
         c.start()
@@ -118,9 +123,11 @@
         c.wait()
 
 
-def unet_kernel(own_ref, left_ref, right_ref, anti_ref, k1, k2, kd, kc, ku, km, kp, out_ref,
-                xf, x1, x2, x3, xc, xu, w1, w2, wd, wc, wu, wma, wmb, wp):
-    height, channels, cols = own_ref.shape
+def unet_kernel(own_ref, left_ref, right_ref, anti_ref, anti_left_ref, anti_right_ref, k1, k2, kd, kc, ku, km, kp, out_ref,
+                xf, x1, x2, x3, xc, xu, w1, wlast, wfirst, wnext, w2, wd, wc, wu, wma, wmb, wp):
+    groups, cols, wide = own_ref.shape
+    height = groups * PER
+    channels = wide // PER
     half = cols // 2
     J = half + 2 * HALO
     C = k1.shape[2]
@@ -129,7 +136,7 @@
     pairs = height // 2
     AB = pairs + 1
 
-    for w in (w1, w2, wd, wc, wu, wma, wmb, wp):
+    for w in (w1, wlast, wfirst, wnext, w2, wd, wc, wu, wma, wmb, wp):
         w[...] = jnp.zeros_like(w)
 
     def fill(w, kernel, cin, first_in):
@@ -143,7 +150,22 @@
                             lane = a * 4 * cin + l * cin
                             w[at : at + C, lane : lane + cin] = kernel[kr, kcol][:, first_in : first_in + cin]
 
-    fill(w1, k1, channels, 0)
+    for p in range(2):
+        for l, off in enumerate(OFFSETS):
+            if not 0 <= off - p + 1 < 3:
+                continue
+            k = [k1[kr, off - p + 1] for kr in range(3)]
+            lane = l * wide
+            for r in range(PER):
+                at = (r * 2 + p) * C
+                for kr in range(3):
+                    if 0 <= r + kr - 1 < PER:
+                        to = lane + (r + kr - 1) * channels
+                        w1[at : at + C, to : to + channels] = k[kr]
+            end = lane + (PER - 1) * channels
+            wlast[p * C : (p + 1) * C, end : end + channels] = k[0]
+            wfirst[p * C : (p + 1) * C, lane : lane + channels] = k[0]
+            wnext[p * C : (p + 1) * C, lane : lane + channels] = k[2]
     fill(w2, k2, C, 0)
     fill(wma, km, C, 0)
     fill(wmb, km, C, C)
@@ -163,34 +185,13 @@
         wp[g * COUT : (g + 1) * COUT, g * C : (g + 1) * C] = kp[...].astype(F32)
 
     def spread(g, l, r):
-        lane = lax.broadcasted_iota(jnp.int32, g.shape, 1)
-        even = jnp.where(lane < half, g, jnp.where(lane < half + HALO, pltpu.roll(r, half, 1), pltpu.roll(l, 2 * HALO, 1)))
-        odd = jnp.where(lane < half, pltpu.roll(g, half, 1),
-                        jnp.where(lane < half + HALO, r, pltpu.roll(l, half + 2 * HALO, 1)))
-        after = jnp.where(lane == J - 1, pltpu.roll(even, J - 1, 1), pltpu.roll(even, cols - 1, 1))
-        before = jnp.where(lane == 0, pltpu.roll(odd, cols - J + 1, 1), pltpu.roll(odd, 1, 1))
-        return jnp.concatenate([even, odd, after, before], axis=0)
-
-    tap = 4 * channels
-
-    def put(slot, value):
-        i, a = slot // 2, slot % 2
-        if i < xf.shape[0]:
-            xf[i, :, a * tap : (a + 1) * tap] = value
-        if i > 0:
-            xf[i - 1, :, (a + 2) * tap : (a + 3) * tap] = value
-
-    for h in range(height):
-        value = spread(own_ref[h].astype(F32), left_ref[h].astype(F32), right_ref[h].astype(F32)).T[:J].astype(BF16)
-        put(h + 1, value)
-        if h == 0:
-            put(height + 2, value)
-    for h in range(POLE - 1):
-        value = spread(anti_ref[0, h].astype(F32), anti_ref[1, h].astype(F32), anti_ref[2, h].astype(F32)).T[:J].astype(BF16)
-        put(height + 3 + h, value)
-        if h == 0:
-            put(0, value)
-    put(height + 1, jnp.zeros((J, tap), BF16))
+        even = jnp.concatenate([g[:half], r[:HALO], l[:HALO]], axis=0)
+        odd = jnp.concatenate([g[half:], r[HALO:], l[HALO:]], axis=0)
+        return jnp.concatenate([even, odd, pltpu.roll(even, J - 1, 0), pltpu.roll(odd, 1, 0)], axis=1).astype(BF16)
+
+    for g in range(groups):
+        xf[g] = spread(own_ref[g].astype(F32), left_ref[g].astype(F32), right_ref[g].astype(F32))
+    xf[groups] = spread(anti_ref[...].astype(F32), anti_left_ref[...].astype(F32), anti_right_ref[...].astype(F32))
 
     def neighbours(v):
         count = v.shape[0]
@@ -212,19 +213,28 @@
         v = x[pl.ds(i0 + a // 2, count), a % 2, 0:width]
         return v.reshape(count * width, v.shape[-1])
 
+    B = pairs
+
     def own_loop(steps, body):
-        def run(t, carry):
+        for t in range(steps):
             body(t)
-            return carry
-        lax.fori_loop(0, steps, run, 0)
-
-    B = 4
-
-    def first(i0, count):
-        store_pair(x1, i0, count, silu(dot_nt(xf[pl.ds(i0, count)].reshape(count * J, 4 * tap), w1[...])))
-
-    first(AB, 3)
-    own_loop(pairs // B, lambda t: first(t * B, B))
+
+    every = groups + 1
+    acc = dot_nt(xf[...].reshape(every * J, 4 * wide), w1[...]).reshape(every, J, PER * 2 * C)
+    from_last = dot_nt(xf[pl.ds(0, groups - 1)].reshape((groups - 1) * J, 4 * wide), wlast[...]).reshape(groups - 1, J, 2 * C)
+    from_next = dot_nt(xf[pl.ds(1, groups - 1)].reshape((groups - 1) * J, 4 * wide), wnext[...]).reshape(groups - 1, J, 2 * C)
+    own_top = dot_nt(xf[groups], wfirst[...])
+    anti_top = dot_nt(xf[0], wfirst[...])
+    for g in range(every):
+        for r in range(PER):
+            v = acc[g, :, r * 2 * C : (r + 1) * 2 * C]
+            if r == 0:
+                v = v + (anti_top if g == groups else own_top if g == 0 else from_last[g - 1])
+            if r == PER - 1 and g < groups - 1:
+                v = v + from_next[g]
+            slot = g * PER + r + 1 + (2 if g == groups else 0)
+            if slot // 2 < x1.shape[0]:
+                x1[slot // 2, slot % 2] = neighbours(silu(v))[0]
     wrap(x1)
 
     def second(i0, count):
@@ -295,11 +305,14 @@
         merged = silu(acc).astype(BF16)
         update = dot_nt(wpb, merged)
         lines = []
+        plain = [own_ref[g].astype(F32).T for g in range(groups)]
         for b in range(B):
             u = update[:, b * half : (b + 1) * half]
             for q in range(2):
                 line = jnp.concatenate([u[2 * q * COUT : (2 * q + 1) * COUT], u[(2 * q + 1) * COUT : (2 * q + 2) * COUT]], axis=1)
-                lines.append(line + own_ref[2 * (i0 + b) + q].astype(F32)[:COUT])
+                h = 2 * (i0 + b) + q
+                at = (h % PER) * channels
+                lines.append(line + plain[h // PER][at : at + COUT])
         woven = jnp.dot(jnp.concatenate(lines, axis=0), unperm, precision=lax.Precision.HIGHEST, preferred_element_type=F32)
         for m in range(2 * B):
             out_ref[:, 2 * i0 + m, :] = woven[m * COUT : (m + 1) * COUT]
@@ -311,14 +324,18 @@
     height, cols = table.shape[1], table.shape[2]
     lat = jnp.swapaxes(latlon, 0, 1).reshape(sub_rows * channels, width)
     vm = pl.BlockSpec(memory_space=pltpu.VMEM)
-    field = jax.ShapeDtypeStruct((height, channels, cols), BF16)
-    own, left, right, anti = pl.pallas_call(
+    groups = height // PER
+    edges = jax.ShapeDtypeStruct((groups, 2 * HALO, PER * channels), BF16)
+    corner = jax.ShapeDtypeStruct((2 * HALO, PER * channels), BF16)
+    remapped = pl.pallas_call(
         functools.partial(exchange_kernel, n),
-        out_shape=(field, field, field, jax.ShapeDtypeStruct((3, POLE, channels, cols), BF16)),
+        out_shape=(jax.ShapeDtypeStruct((groups, cols, PER * channels), BF16), edges, edges,
+                   jax.ShapeDtypeStruct((cols, PER * channels), BF16), corner, corner),
         in_specs=[vm] * 2,
-        out_specs=(vm,) * 4,
+        out_specs=(vm,) * 6,
         scratch_shapes=[
             pltpu.VMEM((n, sub_rows * channels, cols), BF16),
+            pltpu.VMEM((2, groups, 2 * HALO, PER * channels), BF16),
             pltpu.SemaphoreType.DMA((n - 1,)),
             pltpu.SemaphoreType.DMA((n - 1,)),
             pltpu.SemaphoreType.DMA,
@@ -334,16 +351,19 @@
     return pl.pallas_call(
         unet_kernel,
         out_shape=jax.ShapeDtypeStruct((COUT, height, cols), F32),
-        in_specs=[vm] * 11,
+        in_specs=[vm] * 13,
         out_specs=vm,
         scratch_shapes=[
-            pltpu.VMEM((pairs + 4, J, 16 * channels), BF16),
+            pltpu.VMEM((height // PER + 1, J, 4 * PER * channels), BF16),
             pltpu.VMEM((pairs + 5, 2, J, 4 * C), BF16),
             pltpu.VMEM((pairs + 4, 2, J, 4 * C), BF16),
             pltpu.VMEM((pairs + 1, 2, J, 4 * C), BF16),
             pltpu.VMEM((pairs + 5, J, 3 * C2), BF16),
             pltpu.VMEM((pairs + 2, J, 2 * C2), BF16),
-            pltpu.VMEM((4 * C, 16 * channels), BF16),
+            pltpu.VMEM((2 * C * PER, 4 * PER * channels), BF16),
+            pltpu.VMEM((2 * C, 4 * PER * channels), BF16),
+            pltpu.VMEM((2 * C, 4 * PER * channels), BF16),
+            pltpu.VMEM((2 * C, 4 * PER * channels), BF16),
             pltpu.VMEM((4 * C, 16 * C), BF16),
             pltpu.VMEM((C2, 12 * C), BF16),
             pltpu.VMEM((C2, 9 * C2), BF16),
@@ -354,7 +374,7 @@
         ],
         compiler_params=pltpu.CompilerParams(vmem_limit_bytes=48 * 2**20),
         name="unet",
-    )(own, left, right, anti, k1, k2, kd, kc, ku, km, kp)
+    )(*remapped, k1, k2, kd, kc, ku, km, kp)
 
 
 def solution(mesh):

time: 42.1 us -> 29.1 us (0.69)
  the two profiles are of different devices: /device:TPU:1 before, /device:TPU:0 now
where the time goes in v1:
time: 29.1 us; the launch traced here: 28.9 us
  Pallas kernels  26.7 us (92%)
  local copies, waits for them, and re-layouts  2.12 us (7%)
    pallas_call x1, Pallas kernels, shards(): pl.pallas_call(functools.partial(exchange_kernel, n), out_shape=(jax.Shap...  17.4 us
    pallas_call x1, Pallas kernels, shards(): pl.pallas_call(unet_kernel, out_shape=jax.ShapeDtypeStruct((COUT, height,...  9.3 us
    unnamed x18, local copies, waits for them, and re-layouts  1.14 us
    transpose x1, local copies, waits for them, and re-layouts, shards(): lat = jnp.swapaxes(latlon, 0, 1).reshape(sub_rows * channels, width)  0.98 us

profile of v1, /device:TPU:0, one launch (start us, length us, event | category | flops | bytes accessed | tf_op | source)
XLA Modules:
  0.0 28.9 jit_solution(13640365763506056993)
XLA Ops:
  0.0 0.0 copy-start.4
  0.0 0.0 copy-start.7
  0.0 0.0 copy-start.6
  0.0 1.0 %copy.10 = bf16[2,16,2048]{2,1,0:T(8,128)(2,1)S(1)} copy(bf16[2,16,2048]{2,0,1:T(2,128)(2,1)} %bitcast.3) | data formatting | bytes 262144 | tf_op jit(solution)/shard_map/transpose | solution.py:325
  1.0 0.0 copy-done.4
  1.0 0.0 copy-start.3
  1.0 17.4 %exchange.1 = (bf16[4,128,128]{2,1,0:T(8,128)(2,1)S(1)}, bf16[4,16,128]{2,1,0:T(8,128)(2,1)S(1)}, bf16[4,16,128]{2,1,0:T(8,128)(2,1)S(1)}, bf16[128,128]{1,0:T(8...) custom-call(bf16[32,2048]{1,0:T(8,128)(2,1)S(1)} %bitcast.2, s32[2,32,128]{2,1,0:T(8,128)S(1)} %copy-done.4), custom_call_target="tpu_custom_call" | custom-call | tf_op jit(solution)/shard_map/exchange/pallas_call | solution.py:330
  18.5 0.0 copy-done.7
  18.5 0.0 copy-start
  18.5 0.1 copy.11.k1
  18.6 0.0 copy-done.6
  18.6 0.0 copy-start.1
  18.6 0.0 copy-start.2
  18.6 0.0 copy-start.5
  18.7 0.2 copy.12.kd
  18.9 0.0 copy-done.3
  18.9 0.5 %copy-done = bf16[3,3,128,128]{3,2,1,0:T(8,128)(2,1)S(1)} copy-done((bf16[3,3,128,128]{3,2,1,0:T(8,128)(2,1)S(1)}, bf16[3,3,128,128]{3,2,1,0:T(8,128)(2,1)}, u32[]{:S(2)}) %copy-start) | copy-done | bytes 294936
  19.4 0.1 copy-done.1
  19.6 0.1 copy-done.2
  19.6 0.0 copy-done.5
  19.6 9.3 %unet.1 = f32[8,32,128]{2,1,0:T(8,128)} custom-call(bf16[4,128,128]{2,1,0:T(8,128)(2,1)S(1)} %get-tuple-element.11.own_ref, bf16[4,16,128]{2,1,0:T(8,128)(2,1)S(1)} %get-tuple-element.12.left_ref, bf16[4,16,128]{2,1,0:T(8,128)(2,1)S(1)} %get-tuple-element.13.right_ref, bf16[128,128]{1,0:T(8,128)(2,1)S(1)} %get-tuple-element.14.anti_ref, ...), custom_call_target="tpu_custom_call" | custom-call | tf_op jit(solution)/shard_map/unet/pallas_call | solution.py:351
Async XLA Ops:
  0.0 1.0 %copy-start.4 = (s32[2,32,128]{2,1,0:T(8,128)S(1)}, s32[2,32,128]{2,1,0:T(8,128)}, u32[]{:S(2)}) copy-start(s32[2,32,128]{2,1,0:T(8,128)} %tab_ref.1) | copy-start | bytes 98308
  0.0 18.5 %copy-start.7 = (bf16[3,3,64,16]{2,3,1,0:T(8,128)(2,1)S(1)}, bf16[3,3,64,16]{2,3,1,0:T(8,128)(2,1)}, u32[]{:S(2)}) copy-start(bf16[3,3,64,16]{2,3,1,0:T(8,128)(2,1)} %param.11) | copy-start | bytes 55300
  0.0 18.6 %copy-start.6 = (bf16[3,3,128,64]{2,3,1,0:T(8,128)(2,1)S(1)}, bf16[3,3,128,64]{2,3,1,0:T(8,128)(2,1)}, u32[]{:S(2)}) copy-start(bf16[3,3,128,64]{2,3,1,0:T(8,128)(2,1)} %param.13) | copy-start | bytes 442372
  1.0 17.9 %copy-start.3 = (bf16[3,3,64,128]{3,2,1,0:T(8,128)(2,1)S(1)}, bf16[3,3,64,128]{3,2,1,0:T(8,128)(2,1)}, u32[]{:S(2)}) copy-start(bf16[3,3,64,128]{3,2,1,0:T(8,128)(2,1)} %km.1) | copy-start | bytes 442372
  18.5 1.0 %copy-start = (bf16[3,3,128,128]{3,2,1,0:T(8,128)(2,1)S(1)}, bf16[3,3,128,128]{3,2,1,0:T(8,128)(2,1)}, u32[]{:S(2)}) copy-start(bf16[3,3,128,128]{3,2,1,0:T(8,128)(2,1)} %kc.1) | copy-start | bytes 884740
  18.6 0.9 %copy-start.1 = (bf16[3,3,64,64]{3,2,1,0:T(8,128)(2,1)S(1)}, bf16[3,3,64,64]{3,2,1,0:T(8,128)(2,1)}, u32[]{:S(2)}) copy-start(bf16[3,3,64,64]{3,2,1,0:T(8,128)(2,1)} %k2.1) | copy-start | bytes 221188
  18.6 1.0 %copy-start.2 = (bf16[3,3,64,128]{3,2,1,0:T(8,128)(2,1)S(1)}, bf16[3,3,64,128]{3,2,1,0:T(8,128)(2,1)}, u32[]{:S(2)}) copy-start(bf16[3,3,64,128]{3,2,1,0:T(8,128)(2,1)} %ku.1) | copy-start | bytes 442372
  18.6 1.0 %copy-start.5 = (bf16[8,64]{1,0:T(8,128)(2,1)S(1)}, bf16[8,64]{1,0:T(8,128)(2,1)}, u32[]{:S(2)}) copy-start(bf16[8,64]{1,0:T(8,128)(2,1)} %kp.1) | copy-start | bytes 3076

commit v2 on v1

--- a/solution.py
+++ b/solution.py
@@ -25,131 +25,28 @@
     return half * jnp.tanh(half) + half
 
 
-def exchange_kernel(n, lat_ref, tab_ref, own_ref, left_ref, right_ref, anti_ref, anti_left_ref, anti_right_ref,
-                    recv, edge, send_sem, recv_sem, own_sem, hsend, hrecv):
-    me = lax.axis_index("lon")
-    group = lax.axis_index("groups")
-    cols = recv.shape[2]
-    height = tab_ref.shape[1]
-    per = height // own_ref.shape[0]
-    channels = own_ref.shape[2] // per
-    barrier = pltpu.get_barrier_semaphore()
-
-    def greet(d, carry):
-        pl.semaphore_signal(barrier, inc=1, device_id=(group, lax.rem(me + d, n)), device_id_type=MESH)
-        return carry
-
-    lax.fori_loop(1, n, greet, 0)
-    mine = pltpu.make_async_copy(lat_ref.at[:, pl.ds(pl.multiple_of(me * cols, cols), cols)], recv.at[me], own_sem)
-    mine.start()
-    pl.semaphore_wait(barrier, n - 1)
-
-    def block_copy(d, slot):
-        target = lax.rem(me + d, n)
-        return pltpu.make_async_remote_copy(
-            src_ref=lat_ref.at[:, pl.ds(pl.multiple_of(target * cols, cols), cols)],
-            dst_ref=recv.at[slot],
-            send_sem=send_sem.at[d - 1],
-            recv_sem=recv_sem.at[d - 1],
-            device_id=(group, target),
-            device_id_type=MESH,
-        )
-
-    def send(d, carry):
-        block_copy(d, me).start()
-        return carry
-
-    lax.fori_loop(1, n, send, 0)
-
-    p = lax.broadcasted_iota(jnp.int32, (cols, cols), 0)
-    w = lax.broadcasted_iota(jnp.int32, (cols, cols), 1)
-    half = cols // 2
-    perm = (w == jnp.where(p < half, 2 * p, 2 * p - cols + 1)).astype(F32).astype(BF16)
-    rows_at = dot_nt(perm, tab_ref[0].astype(F32).astype(BF16)).astype(jnp.int32)
-    cols_at = dot_nt(perm, (tab_ref[1] - me * cols).astype(F32).astype(BF16)).astype(jnp.int32)
-    wide = per * channels
-    lane = lax.broadcasted_iota(jnp.int32, (cols, wide), 1)
-    hots = [(cols_at[:, h : h + 1] == w).astype(F32).astype(BF16) for h in range(height)]
-    at_row = [jnp.broadcast_to(rows_at[:, h : h + 1], (cols, wide)) - lane // channels for h in range(height)]
-    fi = lax.broadcasted_iota(jnp.int32, (per * wide, wide), 0)
-    fo = lax.broadcasted_iota(jnp.int32, (per * wide, wide), 1)
-    fold = ((fi // wide == fo // channels) & (fi % channels == fo % channels)).astype(F32).astype(BF16)
-
-    mine.wait()
-
-    def receive(d, carry):
-        block_copy(d, lax.rem(me - d + n, n)).wait_recv()
-        return carry
-
-    lax.fori_loop(1, n, receive, 0)
-
-    source = recv[...].reshape(n * lat_ref.shape[0], cols)
-    tiles = source.shape[0] // wide
-    for g in range(own_ref.shape[0]):
-        got = dot_nt(jnp.concatenate(hots[g * per : (g + 1) * per], axis=0), source)
-        picked = []
-        for q in range(per):
-            one = jnp.zeros((cols, wide), F32)
-            for t in range(tiles):
-                value = got[q * cols : (q + 1) * cols, t * wide : (t + 1) * wide]
-                one = jnp.where(at_row[g * per + q] == t * per, value, one)
-            picked.append(one.astype(BF16))
-        block = jnp.dot(jnp.concatenate(picked, axis=1), fold, preferred_element_type=F32)
-        own_ref[g] = block.astype(BF16)
-        edge[0, g] = jnp.concatenate([block[0:HALO], block[half : half + HALO]], axis=0).astype(BF16)
-        edge[1, g] = jnp.concatenate([block[half - HALO : half], block[cols - HALO : cols]], axis=0).astype(BF16)
-
-    def halo(k, src, dst, shift):
-        return pltpu.make_async_remote_copy(
-            src_ref=src, dst_ref=dst, send_sem=hsend.at[k], recv_sem=hrecv.at[k],
-            device_id=(group, lax.rem(me + shift + 2 * n, n)), device_id_type=MESH)
-
-    copies = [
-        halo(0, own_ref.at[0], anti_ref, n // 2),
-        halo(1, edge.at[1], left_ref, 1),
-        halo(2, edge.at[0], right_ref, -1),
-        halo(3, edge.at[1, 0], anti_left_ref, n // 2 + 1),
-        halo(4, edge.at[0, 0], anti_right_ref, n // 2 - 1),
-    ]
-    for c in copies:
-        c.start()
-
-    def sent(d, carry):
-        block_copy(d, me).wait_send()
-        return carry
-
-    lax.fori_loop(1, n, sent, 0)
-    for c in copies:
-        c.wait()
-
-
-def unet_kernel(own_ref, left_ref, right_ref, anti_ref, anti_left_ref, anti_right_ref, k1, k2, kd, kc, ku, km, kp, out_ref,
-                xf, x1, x2, x3, xc, xu, w1, wlast, wfirst, wnext, w2, wd, wc, wu, wma, wmb, wp):
-    groups, cols, wide = own_ref.shape
-    height = groups * PER
-    channels = wide // PER
-    half = cols // 2
-    J = half + 2 * HALO
-    C = k1.shape[2]
-    C2 = kd.shape[2]
-    COUT = kp.shape[0]
-    pairs = height // 2
-    AB = pairs + 1
-
-    for w in (w1, wlast, wfirst, wnext, w2, wd, wc, wu, wma, wmb, wp):
+def clear(*arrays):
+    for w in arrays:
         w[...] = jnp.zeros_like(w)
 
-    def fill(w, kernel, cin, first_in):
-        for q in range(2):
-            for p in range(2):
-                for a in range(4):
-                    for l, off in enumerate(OFFSETS):
-                        kr, kcol = a - q, off - p + 1
-                        if 0 <= kr < 3 and 0 <= kcol < 3:
-                            at = (q * 2 + p) * C
-                            lane = a * 4 * cin + l * cin
-                            w[at : at + C, lane : lane + cin] = kernel[kr, kcol][:, first_in : first_in + cin]
-
+
+def fill(w, kernel, cin, first_in):
+    C = kernel.shape[2]
+    for q in range(2):
+        for p in range(2):
+            for a in range(4):
+                for l, off in enumerate(OFFSETS):
+                    kr, kcol = a - q, off - p + 1
+                    if 0 <= kr < 3 and 0 <= kcol < 3:
+                        at = (q * 2 + p) * C
+                        lane = a * 4 * cin + l * cin
+                        w[at : at + C, lane : lane + cin] = kernel[kr, kcol][:, first_in : first_in + cin]
+
+
+def fine_weights(k1, k2, km, w1, wlast, wfirst, wnext, w2, wma, wmb):
+    C, channels = k1.shape[2], k1.shape[3]
+    wide = PER * channels
+    clear(w1, wlast, wfirst, wnext, w2, wma, wmb)
     for p in range(2):
         for l, off in enumerate(OFFSETS):
             if not 0 <= off - p + 1 < 3:
@@ -169,6 +66,12 @@
     fill(w2, k2, C, 0)
     fill(wma, km, C, 0)
     fill(wmb, km, C, C)
+
+
+def coarse_weights(kd, kc, ku, kp, wd, wc, wu, wp):
+    C2, C = kd.shape[2], kd.shape[3]
+    COUT = kp.shape[0]
+    clear(wd, wc, wu, wp)
     for a in range(3):
         for l, kcol in ((0, 1), (1, 2), (3, 0)):
             wd[:, a * 4 * C + l * C : a * 4 * C + (l + 1) * C] = kd[a, kcol]
@@ -183,6 +86,123 @@
                     wu[at : at + C, lane : lane + C2] = ku[kr, kcol]
     for g in range(4):
         wp[g * COUT : (g + 1) * COUT, g * C : (g + 1) * C] = kp[...].astype(F32)
+
+
+def exchange_kernel(n, lat_ref, tab_ref, k1, k2, kd, kc, ku, km, kp,
+                    own_ref, left_ref, right_ref, anti_ref, anti_left_ref, anti_right_ref,
+                    w1, wlast, wfirst, wnext, w2, wd, wc, wu, wma, wmb, wp,
+                    recv, edge, send_sem, recv_sem, own_sem, hsend, hrecv):
+    me = lax.axis_index("lon")
+    group = lax.axis_index("groups")
+    cols = recv.shape[2]
+    height = tab_ref.shape[1]
+    per = height // own_ref.shape[0]
+    channels = own_ref.shape[2] // per
+    barrier = pltpu.get_barrier_semaphore()
+
+    def greet(d, carry):
+        pl.semaphore_signal(barrier, inc=1, device_id=(group, lax.rem(me + d, n)), device_id_type=MESH)
+        return carry
+
+    lax.fori_loop(1, n, greet, 0)
+    mine = pltpu.make_async_copy(lat_ref.at[:, pl.ds(pl.multiple_of(me * cols, cols), cols)], recv.at[me], own_sem)
+    mine.start()
+    coarse_weights(kd, kc, ku, kp, wd, wc, wu, wp)
+    pl.semaphore_wait(barrier, n - 1)
+
+    def block_copy(d, slot):
+        target = lax.rem(me + d, n)
+        return pltpu.make_async_remote_copy(
+            src_ref=lat_ref.at[:, pl.ds(pl.multiple_of(target * cols, cols), cols)],
+            dst_ref=recv.at[slot],
+            send_sem=send_sem.at[d - 1],
+            recv_sem=recv_sem.at[d - 1],
+            device_id=(group, target),
+            device_id_type=MESH,
+        )
+
+    def send(d, carry):
+        block_copy(d, me).start()
+        return carry
+
+    lax.fori_loop(1, n, send, 0)
+
+    fine_weights(k1, k2, km, w1, wlast, wfirst, wnext, w2, wma, wmb)
+
+    p = lax.broadcasted_iota(jnp.int32, (cols, cols), 0)
+    w = lax.broadcasted_iota(jnp.int32, (cols, cols), 1)
+    half = cols // 2
+    perm = (w == jnp.where(p < half, 2 * p, 2 * p - cols + 1)).astype(F32).astype(BF16)
+    rows_at = dot_nt(perm, tab_ref[0].astype(F32).astype(BF16)).astype(jnp.int32)
+    cols_at = dot_nt(perm, (tab_ref[1] - me * cols).astype(F32).astype(BF16)).astype(jnp.int32)
+    wide = per * channels
+    lane = lax.broadcasted_iota(jnp.int32, (cols, wide), 1)
+    hots = [(cols_at[:, h : h + 1] == w).astype(F32).astype(BF16) for h in range(height)]
+    at_row = [jnp.broadcast_to(rows_at[:, h : h + 1], (cols, wide)) - lane // channels for h in range(height)]
+    fi = lax.broadcasted_iota(jnp.int32, (per * wide, wide), 0)
+    fo = lax.broadcasted_iota(jnp.int32, (per * wide, wide), 1)
+    fold = ((fi // wide == fo // channels) & (fi % channels == fo % channels)).astype(F32).astype(BF16)
+
+    mine.wait()
+
+    def receive(d, carry):
+        block_copy(d, lax.rem(me - d + n, n)).wait_recv()
+        return carry
+
+    lax.fori_loop(1, n, receive, 0)
+
+    source = recv[...].reshape(n * lat_ref.shape[0], cols)
+    tiles = source.shape[0] // wide
+    for g in range(own_ref.shape[0]):
+        got = dot_nt(jnp.concatenate(hots[g * per : (g + 1) * per], axis=0), source)
+        picked = []
+        for q in range(per):
+            one = jnp.zeros((cols, wide), F32)
+            for t in range(tiles):
+                value = got[q * cols : (q + 1) * cols, t * wide : (t + 1) * wide]
+                one = jnp.where(at_row[g * per + q] == t * per, value, one)
+            picked.append(one.astype(BF16))
+        block = jnp.dot(jnp.concatenate(picked, axis=1), fold, preferred_element_type=F32)
+        own_ref[g] = block.astype(BF16)
+        edge[0, g] = jnp.concatenate([block[0:HALO], block[half : half + HALO]], axis=0).astype(BF16)
+        edge[1, g] = jnp.concatenate([block[half - HALO : half], block[cols - HALO : cols]], axis=0).astype(BF16)
+
+    def halo(k, src, dst, shift):
+        return pltpu.make_async_remote_copy(
+            src_ref=src, dst_ref=dst, send_sem=hsend.at[k], recv_sem=hrecv.at[k],
+            device_id=(group, lax.rem(me + shift + 2 * n, n)), device_id_type=MESH)
+
+    copies = [
+        halo(0, own_ref.at[0], anti_ref, n // 2),
+        halo(1, edge.at[1], left_ref, 1),
+        halo(2, edge.at[0], right_ref, -1),
+        halo(3, edge.at[1, 0], anti_left_ref, n // 2 + 1),
+        halo(4, edge.at[0, 0], anti_right_ref, n // 2 - 1),
+    ]
+    for c in copies:
+        c.start()
+
+    def sent(d, carry):
+        block_copy(d, me).wait_send()
+        return carry
+
+    lax.fori_loop(1, n, sent, 0)
+    for c in copies:
+        c.wait()
+
+
+def unet_kernel(own_ref, left_ref, right_ref, anti_ref, anti_left_ref, anti_right_ref,
+                w1, wlast, wfirst, wnext, w2, wd, wc, wu, wma, wmb, wp, out_ref, xf, x1, x2, x3, xc, xu):
+    groups, cols, wide = own_ref.shape
+    height = groups * PER
+    channels = wide // PER
+    half = cols // 2
+    J = half + 2 * HALO
+    C = w2.shape[0] // 4
+    C2 = wd.shape[0]
+    COUT = wp.shape[0] // 4
+    pairs = height // 2
+    AB = pairs + 1
 
     def spread(g, l, r):
         even = jnp.concatenate([g[:half], r[:HALO], l[:HALO]], axis=0)
@@ -327,12 +347,26 @@
     groups = height // PER
     edges = jax.ShapeDtypeStruct((groups, 2 * HALO, PER * channels), BF16)
     corner = jax.ShapeDtypeStruct((2 * HALO, PER * channels), BF16)
-    remapped = pl.pallas_call(
+    C, C2, COUT = k1.shape[2], kd.shape[2], kp.shape[0]
+    weights = (
+        jax.ShapeDtypeStruct((2 * C * PER, 4 * PER * channels), BF16),
+        jax.ShapeDtypeStruct((2 * C, 4 * PER * channels), BF16),
+        jax.ShapeDtypeStruct((2 * C, 4 * PER * channels), BF16),
+        jax.ShapeDtypeStruct((2 * C, 4 * PER * channels), BF16),
+        jax.ShapeDtypeStruct((4 * C, 16 * C), BF16),
+        jax.ShapeDtypeStruct((C2, 12 * C), BF16),
+        jax.ShapeDtypeStruct((C2, 9 * C2), BF16),
+        jax.ShapeDtypeStruct((4 * C, 4 * C2), BF16),
+        jax.ShapeDtypeStruct((4 * C, 16 * C), BF16),
+        jax.ShapeDtypeStruct((4 * C, 16 * C), BF16),
+        jax.ShapeDtypeStruct((4 * COUT, 4 * C), F32),
+    )
+    ready = pl.pallas_call(
         functools.partial(exchange_kernel, n),
         out_shape=(jax.ShapeDtypeStruct((groups, cols, PER * channels), BF16), edges, edges,
-                   jax.ShapeDtypeStruct((cols, PER * channels), BF16), corner, corner),
-        in_specs=[vm] * 2,
-        out_specs=(vm,) * 6,
+                   jax.ShapeDtypeStruct((cols, PER * channels), BF16), corner, corner) + weights,
+        in_specs=[vm] * 9,
+        out_specs=(vm,) * 17,
         scratch_shapes=[
             pltpu.VMEM((n, sub_rows * channels, cols), BF16),
             pltpu.VMEM((2, groups, 2 * HALO, PER * channels), BF16),
@@ -342,16 +376,15 @@
             pltpu.SemaphoreType.DMA((5,)),
             pltpu.SemaphoreType.DMA((5,)),
         ],
-        compiler_params=pltpu.CompilerParams(collective_id=0, has_side_effects=True, vmem_limit_bytes=48 * 2**20),
+        compiler_params=pltpu.CompilerParams(collective_id=0, has_side_effects=True, vmem_limit_bytes=32 * 2**20),
         name="exchange",
-    )(lat, table)
-    C, C2, COUT = k1.shape[2], kd.shape[2], kp.shape[0]
+    )(lat, table, k1, k2, kd, kc, ku, km, kp)
     J = cols // 2 + 2 * HALO
     pairs = height // 2
     return pl.pallas_call(
         unet_kernel,
         out_shape=jax.ShapeDtypeStruct((COUT, height, cols), F32),
-        in_specs=[vm] * 13,
+        in_specs=[vm] * 17,
         out_specs=vm,
         scratch_shapes=[
             pltpu.VMEM((height // PER + 1, J, 4 * PER * channels), BF16),
@@ -360,21 +393,10 @@
             pltpu.VMEM((pairs + 1, 2, J, 4 * C), BF16),
             pltpu.VMEM((pairs + 5, J, 3 * C2), BF16),
             pltpu.VMEM((pairs + 2, J, 2 * C2), BF16),
-            pltpu.VMEM((2 * C * PER, 4 * PER * channels), BF16),
-            pltpu.VMEM((2 * C, 4 * PER * channels), BF16),
-            pltpu.VMEM((2 * C, 4 * PER * channels), BF16),
-            pltpu.VMEM((2 * C, 4 * PER * channels), BF16),
-            pltpu.VMEM((4 * C, 16 * C), BF16),
-            pltpu.VMEM((C2, 12 * C), BF16),
-            pltpu.VMEM((C2, 9 * C2), BF16),
-            pltpu.VMEM((4 * C, 4 * C2), BF16),
-            pltpu.VMEM((4 * C, 16 * C), BF16),
-            pltpu.VMEM((4 * C, 16 * C), BF16),
-            pltpu.VMEM((4 * COUT, 4 * C), F32),
         ],
-        compiler_params=pltpu.CompilerParams(vmem_limit_bytes=48 * 2**20),
+        compiler_params=pltpu.CompilerParams(vmem_limit_bytes=32 * 2**20),
         name="unet",
-    )(*remapped, k1, k2, kd, kc, ku, km, kp)
+    )(*ready)
 
 
 def solution(mesh):

time: 29.1 us -> 28.2 us (0.969)
  Pallas kernels: 26.7 us -> 25.6 us
    pallas_call x1, Pallas kernels: 9.3 us -> 8.12 us  [shards(): pl.pallas_call(unet_kernel, out_shape=jax.ShapeDtypeStruct((COUT, height,...]
    unnamed x18 -> x16, local copies, waits for them, and re-layouts: 1.14 us -> 1.37 us
where the time goes in v2:
time: 28.2 us; the launch traced here: 28 us
  Pallas kernels  25.6 us (91%)
  local copies, waits for them, and re-layouts  2.35 us (8%)
    pallas_call x1, Pallas kernels, shards(): pl.pallas_call(functools.partial(exchange_kernel, n), out_shape=(jax.Shap...  17.4 us
    pallas_call x1, Pallas kernels, shards(): pl.pallas_call(unet_kernel, out_shape=jax.ShapeDtypeStruct((COUT, height,...  8.12 us
    unnamed x16, local copies, waits for them, and re-layouts  1.37 us
    transpose x1, local copies, waits for them, and re-layouts, shards(): lat = jnp.swapaxes(latlon, 0, 1).reshape(sub_rows * channels, width)  0.98 us

profile of v2, /device:TPU:0, one launch (start us, length us, event | category | flops | bytes accessed | tf_op | source)
XLA Modules:
  0.0 28.0 jit_solution(16266377639301646827)
XLA Ops:
  0.0 0.0 copy-start.6
  0.0 0.0 copy-start.3
  0.0 1.0 %copy.10 = bf16[2,16,2048]{2,1,0:T(8,128)(2,1)S(1)} copy(bf16[2,16,2048]{2,0,1:T(2,128)(2,1)} %bitcast.3) | data formatting | bytes 262144 | tf_op jit(solution)/shard_map/transpose | solution.py:345
  1.0 0.0 copy-done.6
  1.0 0.0 copy-start
  1.0 0.1 copy.11.k1
  1.2 0.0 copy-start.1
  1.2 0.0 copy-start.2
  1.2 0.0 copy-start.4
  1.2 0.0 copy-start.5
  1.2 1.2 %copy.12.kd = bf16[3,3,128,64]{3,2,1,0:T(8,128)(2,1)S(1)} copy(bf16[3,3,128,64]{2,3,1,0:T(8,128)(2,1)} %param.13) | data formatting | bytes 294912 | tf_op args[4]
  2.4 0.0 copy-done.3
  2.4 0.0 copy-done
  2.4 0.0 copy-done.1
  2.4 0.0 copy-done.2
  2.4 0.0 copy-done.4
  2.4 0.0 copy-done.5
  2.4 17.4 %exchange.1 = (bf16[4,128,128]{2,1,0:T(8,128)(2,1)S(1)}, bf16[4,16,128]{2,1,0:T(8,128)(2,1)S(1)}, bf16[4,16,128]{2,1,0:T(8,128)(2,1)S(1)}, bf16[128,128]{1,0:T(8...) custom-call(bf16[32,2048]{1,0:T(8,128)(2,1)S(1)} %bitcast.2, ...), custom_call_target="tpu_custom_call" | custom-call | tf_op jit(solution)/shard_map/exchange/pallas_call | solution.py:364
  19.9 8.1 %unet.1 = f32[8,32,128]{2,1,0:T(8,128)} custom-call(bf16[4,128,128]{2,1,0:T(8,128)(2,1)S(1)} %get-tuple-element.22.own_ref, bf16[4,16,128]{2,1,0:T(8,128)(2,1)S(1)} %get-tuple-element.23.left_ref, bf16[4,16,128]{2,1,0:T(8,128)(2,1)S(1)} %get-tuple-element.24.right_ref, bf16[128,128]{1,0:T(8,128)(2,1)S(1)} %get-tuple-element.25.anti_ref, ...), custom_call_target="tpu_custom_call" | custom-call | tf_op jit(solution)/shard_map/unet/pallas_call | solution.py:384
Async XLA Ops:
  0.0 1.0 %copy-start.6 = (bf16[3,3,64,16]{2,3,1,0:T(8,128)(2,1)S(1)}, bf16[3,3,64,16]{2,3,1,0:T(8,128)(2,1)}, u32[]{:S(2)}) copy-start(bf16[3,3,64,16]{2,3,1,0:T(8,128)(2,1)} %param.11) | copy-start | bytes 55300
  0.0 2.4 %copy-start.3 = (bf16[3,3,64,128]{3,2,1,0:T(8,128)(2,1)S(1)}, bf16[3,3,64,128]{3,2,1,0:T(8,128)(2,1)}, u32[]{:S(2)}) copy-start(bf16[3,3,64,128]{3,2,1,0:T(8,128)(2,1)} %km.1) | copy-start | bytes 442372
  1.0 1.4 %copy-start = (bf16[3,3,128,128]{3,2,1,0:T(8,128)(2,1)S(1)}, bf16[3,3,128,128]{3,2,1,0:T(8,128)(2,1)}, u32[]{:S(2)}) copy-start(bf16[3,3,128,128]{3,2,1,0:T(8,128)(2,1)} %kc.1) | copy-start | bytes 884740
  1.2 1.3 %copy-start.1 = (bf16[3,3,64,64]{3,2,1,0:T(8,128)(2,1)S(1)}, bf16[3,3,64,64]{3,2,1,0:T(8,128)(2,1)}, u32[]{:S(2)}) copy-start(bf16[3,3,64,64]{3,2,1,0:T(8,128)(2,1)} %k2.1) | copy-start | bytes 221188
  1.2 1.3 %copy-start.2 = (bf16[3,3,64,128]{3,2,1,0:T(8,128)(2,1)S(1)}, bf16[3,3,64,128]{3,2,1,0:T(8,128)(2,1)}, u32[]{:S(2)}) copy-start(bf16[3,3,64,128]{3,2,1,0:T(8,128)(2,1)} %ku.1) | copy-start | bytes 442372
  1.2 1.3 %copy-start.4 = (s32[2,32,128]{2,1,0:T(8,128)S(1)}, s32[2,32,128]{2,1,0:T(8,128)}, u32[]{:S(2)}) copy-start(s32[2,32,128]{2,1,0:T(8,128)} %tab_ref.1) | copy-start | bytes 98308
  1.2 1.2 %copy-start.5 = (bf16[8,64]{1,0:T(8,128)(2,1)S(1)}, bf16[8,64]{1,0:T(8,128)(2,1)}, u32[]{:S(2)}) copy-start(bf16[8,64]{1,0:T(8,128)(2,1)} %kp.1) | copy-start | bytes 3076

commit v3 on v2

--- a/solution.py
+++ b/solution.py
@@ -44,14 +44,14 @@
 
 
 def fine_weights(k1, k2, km, w1, wlast, wfirst, wnext, w2, wma, wmb):
-    C, channels = k1.shape[2], k1.shape[3]
+    C, channels = k2.shape[2], k1.shape[2]
     wide = PER * channels
     clear(w1, wlast, wfirst, wnext, w2, wma, wmb)
     for p in range(2):
         for l, off in enumerate(OFFSETS):
             if not 0 <= off - p + 1 < 3:
                 continue
-            k = [k1[kr, off - p + 1] for kr in range(3)]
+            k = [k1[kr, off - p + 1].astype(F32).T.astype(BF16) for kr in range(3)]
             lane = l * wide
             for r in range(PER):
                 at = (r * 2 + p) * C
@@ -69,12 +69,12 @@
 
 
 def coarse_weights(kd, kc, ku, kp, wd, wc, wu, wp):
-    C2, C = kd.shape[2], kd.shape[3]
+    C, C2 = kd.shape[2], kd.shape[3]
     COUT = kp.shape[0]
     clear(wd, wc, wu, wp)
     for a in range(3):
         for l, kcol in ((0, 1), (1, 2), (3, 0)):
-            wd[:, a * 4 * C + l * C : a * 4 * C + (l + 1) * C] = kd[a, kcol]
+            wd[:, a * 4 * C + l * C : a * 4 * C + (l + 1) * C] = kd[a, kcol].astype(F32).T.astype(BF16)
         for s, kcol in enumerate((1, 2, 0)):
             wc[:, (a * 3 + s) * C2 : (a * 3 + s + 1) * C2] = kc[a, kcol]
     for q, rows in ((0, ((0, 1),)), (1, ((0, 0), (1, 2)))):
@@ -151,6 +151,18 @@
 
     lax.fori_loop(1, n, receive, 0)
 
+    def halo(k, src, dst, shift):
+        return pltpu.make_async_remote_copy(
+            src_ref=src, dst_ref=dst, send_sem=hsend.at[k], recv_sem=hrecv.at[k],
+            device_id=(group, lax.rem(me + shift + 2 * n, n)), device_id_type=MESH)
+
+    copies = [
+        halo(0, own_ref.at[0], anti_ref, n // 2),
+        halo(1, edge.at[1, 0], anti_left_ref, n // 2 + 1),
+        halo(2, edge.at[0, 0], anti_right_ref, n // 2 - 1),
+        halo(3, edge.at[1], left_ref, 1),
+        halo(4, edge.at[0], right_ref, -1),
+    ]
     source = recv[...].reshape(n * lat_ref.shape[0], cols)
     tiles = source.shape[0] // wide
     for g in range(own_ref.shape[0]):
@@ -166,20 +178,11 @@
         own_ref[g] = block.astype(BF16)
         edge[0, g] = jnp.concatenate([block[0:HALO], block[half : half + HALO]], axis=0).astype(BF16)
         edge[1, g] = jnp.concatenate([block[half - HALO : half], block[cols - HALO : cols]], axis=0).astype(BF16)
-
-    def halo(k, src, dst, shift):
-        return pltpu.make_async_remote_copy(
-            src_ref=src, dst_ref=dst, send_sem=hsend.at[k], recv_sem=hrecv.at[k],
-            device_id=(group, lax.rem(me + shift + 2 * n, n)), device_id_type=MESH)
-
-    copies = [
-        halo(0, own_ref.at[0], anti_ref, n // 2),
-        halo(1, edge.at[1], left_ref, 1),
-        halo(2, edge.at[0], right_ref, -1),
-        halo(3, edge.at[1, 0], anti_left_ref, n // 2 + 1),
-        halo(4, edge.at[0, 0], anti_right_ref, n // 2 - 1),
-    ]
-    for c in copies:
+        if g == 0:
+            for c in copies[:3]:
+                c.start()
+
+    for c in copies[3:]:
         c.start()
 
     def sent(d, carry):
@@ -378,7 +381,7 @@
         ],
         compiler_params=pltpu.CompilerParams(collective_id=0, has_side_effects=True, vmem_limit_bytes=32 * 2**20),
         name="exchange",
-    )(lat, table, k1, k2, kd, kc, ku, km, kp)
+    )(lat, table, jnp.swapaxes(k1, 2, 3), k2, jnp.swapaxes(kd, 2, 3), kc, ku, km, kp)
     J = cols // 2 + 2 * HALO
     pairs = height // 2
     return pl.pallas_call(

time: 28.2 us -> 30.2 us (1.071)
  local copies, waits for them, and re-layouts: 2.35 us -> 4.68 us
  Pallas kernels: 25.6 us -> 25.2 us
    unnamed x16, local copies, waits for them, and re-layouts: 1.37 us -> 3.7 us
where the time goes in v3:
time: 30.2 us; the launch traced here: 30 us
  Pallas kernels  25.2 us (83%)
  local copies, waits for them, and re-layouts  4.68 us (15%)
    pallas_call x1, Pallas kernels, shards(): pl.pallas_call(functools.partial(exchange_kernel, n), out_shape=(jax.Shap...  17.1 us
    pallas_call x1, Pallas kernels, shards(): pl.pallas_call(unet_kernel, out_shape=jax.ShapeDtypeStruct((COUT, height,...  8.11 us
    unnamed x16, local copies, waits for them, and re-layouts  3.7 us
    transpose x1, local copies, waits for them, and re-layouts, shards(): lat = jnp.swapaxes(latlon, 0, 1).reshape(sub_rows * channels, width)  0.98 us

profile of v3, /device:TPU:0, one launch (start us, length us, event | category | flops | bytes accessed | tf_op | source)
XLA Modules:
  0.0 30.0 jit_solution(5866225322153960021)
XLA Ops:
  0.0 0.0 copy-start.1
  0.0 0.0 copy-start.5
  0.0 0.0 copy-start.6
  0.0 0.0 copy-start.7
  0.0 1.0 %copy.10 = bf16[2,16,2048]{2,1,0:T(8,128)(2,1)S(1)} copy(bf16[2,16,2048]{2,0,1:T(2,128)(2,1)} %bitcast.7) | data formatting | bytes 262144 | tf_op jit(solution)/shard_map/transpose | solution.py:348
  1.0 0.0 copy-done.1
  1.0 0.0 copy-done.5
  1.0 0.0 copy-done.6
  1.0 0.0 copy-done.7
  1.0 0.0 copy-start
  1.0 1.0 %copy-done = bf16[3,3,128,128]{3,2,1,0:T(8,128)(2,1)S(1)} copy-done((bf16[3,3,128,128]{3,2,1,0:T(8,128)(2,1)S(1)}, bf16[3,3,128,128]{3,2,1,0:T(8,128)(2,1)}, u32[]{:S(2)}) %copy-start) | copy-done | bytes 294936
  2.0 0.0 copy-start.2
  2.0 0.9 %copy-done.2 = bf16[3,3,128,64]{2,3,1,0:T(8,128)(2,1)S(1)} copy-done((bf16[3,3,128,64]{2,3,1,0:T(8,128)(2,1)S(1)}, bf16[3,3,128,64]{2,3,1,0:T(8,128)(2,1)}, u32[]{:S(2)}) %copy-start.2) | copy-done | bytes 147480
  2.9 0.0 copy-start.3
  2.9 0.9 %copy-done.3 = bf16[3,3,64,128]{3,2,1,0:T(8,128)(2,1)S(1)} copy-done((bf16[3,3,64,128]{3,2,1,0:T(8,128)(2,1)S(1)}, bf16[3,3,64,128]{3,2,1,0:T(8,128)(2,1)}, u32[]{:S(2)}) %copy-start.3) | copy-done | bytes 147480
  3.8 0.0 copy-start.4
  3.8 0.9 %copy-done.4 = bf16[3,3,64,128]{3,2,1,0:T(8,128)(2,1)S(1)} copy-done((bf16[3,3,64,128]{3,2,1,0:T(8,128)(2,1)S(1)}, bf16[3,3,64,128]{3,2,1,0:T(8,128)(2,1)}, u32[]{:S(2)}) %copy-start.4) | copy-done | bytes 147480
  4.7 17.1 %exchange.1 = (bf16[4,128,128]{2,1,0:T(8,128)(2,1)S(1)}, bf16[4,16,128]{2,1,0:T(8,128)(2,1)S(1)}, bf16[4,16,128]{2,1,0:T(8,128)(2,1)S(1)}, bf16[128,128]{1,0:T(8...) custom-call(bf16[32,2048]{1,0:T(8,128)(2,1)S(1)} %bitcast.4, ...), custom_call_target="tpu_custom_call" | custom-call | tf_op jit(solution)/shard_map/exchange/pallas_call | solution.py:367
  21.9 8.1 %unet.1 = f32[8,32,128]{2,1,0:T(8,128)} custom-call(bf16[4,128,128]{2,1,0:T(8,128)(2,1)S(1)} %get-tuple-element.22.own_ref, bf16[4,16,128]{2,1,0:T(8,128)(2,1)S(1)} %get-tuple-element.23.left_ref, bf16[4,16,128]{2,1,0:T(8,128)(2,1)S(1)} %get-tuple-element.24.right_ref, bf16[128,128]{1,0:T(8,128)(2,1)S(1)} %get-tuple-element.25.anti_ref, ...), custom_call_target="tpu_custom_call" | custom-call | tf_op jit(solution)/shard_map/unet/pallas_call | solution.py:387
Async XLA Ops:
  0.0 1.0 %copy-start.1 = (bf16[3,3,64,64]{3,2,1,0:T(8,128)(2,1)S(1)}, bf16[3,3,64,64]{3,2,1,0:T(8,128)(2,1)}, u32[]{:S(2)}) copy-start(bf16[3,3,64,64]{3,2,1,0:T(8,128)(2,1)} %k2.1) | copy-start | bytes 221188
  0.0 1.0 %copy-start.5 = (bf16[3,3,64,16]{2,3,1,0:T(8,128)(2,1)S(1)}, bf16[3,3,64,16]{2,3,1,0:T(8,128)(2,1)}, u32[]{:S(2)}) copy-start(bf16[3,3,64,16]{2,3,1,0:T(8,128)(2,1)} %param.11) | copy-start | bytes 55300
  0.0 1.0 %copy-start.6 = (s32[2,32,128]{2,1,0:T(8,128)S(1)}, s32[2,32,128]{2,1,0:T(8,128)}, u32[]{:S(2)}) copy-start(s32[2,32,128]{2,1,0:T(8,128)} %tab_ref.1) | copy-start | bytes 98308
  0.0 1.0 %copy-start.7 = (bf16[8,64]{1,0:T(8,128)(2,1)S(1)}, bf16[8,64]{1,0:T(8,128)(2,1)}, u32[]{:S(2)}) copy-start(bf16[8,64]{1,0:T(8,128)(2,1)} %kp.1) | copy-start | bytes 3076
  1.0 1.0 %copy-start = (bf16[3,3,128,128]{3,2,1,0:T(8,128)(2,1)S(1)}, bf16[3,3,128,128]{3,2,1,0:T(8,128)(2,1)}, u32[]{:S(2)}) copy-start(bf16[3,3,128,128]{3,2,1,0:T(8,128)(2,1)} %kc.1) | copy-start | bytes 884740
  2.0 0.9 %copy-start.2 = (bf16[3,3,128,64]{2,3,1,0:T(8,128)(2,1)S(1)}, bf16[3,3,128,64]{2,3,1,0:T(8,128)(2,1)}, u32[]{:S(2)}) copy-start(bf16[3,3,128,64]{2,3,1,0:T(8,128)(2,1)} %param.13) | copy-start | bytes 442372
  2.9 0.9 %copy-start.3 = (bf16[3,3,64,128]{3,2,1,0:T(8,128)(2,1)S(1)}, bf16[3,3,64,128]{3,2,1,0:T(8,128)(2,1)}, u32[]{:S(2)}) copy-start(bf16[3,3,64,128]{3,2,1,0:T(8,128)(2,1)} %ku.1) | copy-start | bytes 442372
  3.8 0.9 %copy-start.4 = (bf16[3,3,64,128]{3,2,1,0:T(8,128)(2,1)S(1)}, bf16[3,3,64,128]{3,2,1,0:T(8,128)(2,1)}, u32[]{:S(2)}) copy-start(bf16[3,3,64,128]{3,2,1,0:T(8,128)(2,1)} %km.1) | copy-start | bytes 442372

commit v4 on v3

--- a/solution.py
+++ b/solution.py
@@ -44,14 +44,14 @@
 
 
 def fine_weights(k1, k2, km, w1, wlast, wfirst, wnext, w2, wma, wmb):
-    C, channels = k2.shape[2], k1.shape[2]
+    C, channels = k1.shape[2], k1.shape[3]
     wide = PER * channels
     clear(w1, wlast, wfirst, wnext, w2, wma, wmb)
     for p in range(2):
         for l, off in enumerate(OFFSETS):
             if not 0 <= off - p + 1 < 3:
                 continue
-            k = [k1[kr, off - p + 1].astype(F32).T.astype(BF16) for kr in range(3)]
+            k = [k1[kr, off - p + 1] for kr in range(3)]
             lane = l * wide
             for r in range(PER):
                 at = (r * 2 + p) * C
@@ -69,12 +69,12 @@
 
 
 def coarse_weights(kd, kc, ku, kp, wd, wc, wu, wp):
-    C, C2 = kd.shape[2], kd.shape[3]
+    C2, C = kd.shape[2], kd.shape[3]
     COUT = kp.shape[0]
     clear(wd, wc, wu, wp)
     for a in range(3):
         for l, kcol in ((0, 1), (1, 2), (3, 0)):
-            wd[:, a * 4 * C + l * C : a * 4 * C + (l + 1) * C] = kd[a, kcol].astype(F32).T.astype(BF16)
+            wd[:, a * 4 * C + l * C : a * 4 * C + (l + 1) * C] = kd[a, kcol]
         for s, kcol in enumerate((1, 2, 0)):
             wc[:, (a * 3 + s) * C2 : (a * 3 + s + 1) * C2] = kc[a, kcol]
     for q, rows in ((0, ((0, 1),)), (1, ((0, 0), (1, 2)))):
@@ -381,7 +381,7 @@
         ],
         compiler_params=pltpu.CompilerParams(collective_id=0, has_side_effects=True, vmem_limit_bytes=32 * 2**20),
         name="exchange",
-    )(lat, table, jnp.swapaxes(k1, 2, 3), k2, jnp.swapaxes(kd, 2, 3), kc, ku, km, kp)
+    )(lat, table, k1, k2, kd, kc, ku, km, kp)
     J = cols // 2 + 2 * HALO
     pairs = height // 2
     return pl.pallas_call(

time: 30.2 us -> 27.9 us (0.924)
  local copies, waits for them, and re-layouts: 4.68 us -> 2.35 us
    unnamed x16, local copies, waits for them, and re-layouts: 3.7 us -> 1.37 us
where the time goes in v4:
time: 27.9 us; the launch traced here: 27.8 us
  Pallas kernels  25.3 us (91%)
  local copies, waits for them, and re-layouts  2.35 us (8%)
    pallas_call x1, Pallas kernels, shards(): pl.pallas_call(functools.partial(exchange_kernel, n), out_shape=(jax.Shap...  17.2 us
    pallas_call x1, Pallas kernels, shards(): pl.pallas_call(unet_kernel, out_shape=jax.ShapeDtypeStruct((COUT, height,...  8.12 us
    unnamed x16, local copies, waits for them, and re-layouts  1.37 us
    transpose x1, local copies, waits for them, and re-layouts, shards(): lat = jnp.swapaxes(latlon, 0, 1).reshape(sub_rows * channels, width)  0.98 us

profile of v4, /device:TPU:0, one launch (start us, length us, event | category | flops | bytes accessed | tf_op | source)
XLA Modules:
  0.0 27.8 jit_solution(7168100481449448920)
XLA Ops:
  0.0 0.0 copy-start.6
  0.0 0.0 copy-start.3
  0.0 1.0 %copy.10 = bf16[2,16,2048]{2,1,0:T(8,128)(2,1)S(1)} copy(bf16[2,16,2048]{2,0,1:T(2,128)(2,1)} %bitcast.3) | data formatting | bytes 262144 | tf_op jit(solution)/shard_map/transpose | solution.py:348
  1.0 0.0 copy-done.6
  1.0 0.0 copy-start
  1.0 0.1 copy.11.k1
  1.2 0.0 copy-start.1
  1.2 0.0 copy-start.2
  1.2 0.0 copy-start.4
  1.2 0.0 copy-start.5
  1.2 1.2 %copy.12.kd = bf16[3,3,128,64]{3,2,1,0:T(8,128)(2,1)S(1)} copy(bf16[3,3,128,64]{2,3,1,0:T(8,128)(2,1)} %param.13) | data formatting | bytes 294912 | tf_op args[4]
  2.4 0.0 copy-done.3
  2.4 0.0 copy-done
  2.4 0.0 copy-done.1
  2.4 0.0 copy-done.2
  2.4 0.0 copy-done.4
  2.4 0.0 copy-done.5
  2.4 17.2 %exchange.1 = (bf16[4,128,128]{2,1,0:T(8,128)(2,1)S(1)}, bf16[4,16,128]{2,1,0:T(8,128)(2,1)S(1)}, bf16[4,16,128]{2,1,0:T(8,128)(2,1)S(1)}, bf16[128,128]{1,0:T(8...) custom-call(bf16[32,2048]{1,0:T(8,128)(2,1)S(1)} %bitcast.2, ...), custom_call_target="tpu_custom_call" | custom-call | tf_op jit(solution)/shard_map/exchange/pallas_call | solution.py:367
  19.6 8.1 %unet.1 = f32[8,32,128]{2,1,0:T(8,128)} custom-call(bf16[4,128,128]{2,1,0:T(8,128)(2,1)S(1)} %get-tuple-element.22.own_ref, bf16[4,16,128]{2,1,0:T(8,128)(2,1)S(1)} %get-tuple-element.23.left_ref, bf16[4,16,128]{2,1,0:T(8,128)(2,1)S(1)} %get-tuple-element.24.right_ref, bf16[128,128]{1,0:T(8,128)(2,1)S(1)} %get-tuple-element.25.anti_ref, ...), custom_call_target="tpu_custom_call" | custom-call | tf_op jit(solution)/shard_map/unet/pallas_call | solution.py:387
Async XLA Ops:
  0.0 1.0 %copy-start.6 = (bf16[3,3,64,16]{2,3,1,0:T(8,128)(2,1)S(1)}, bf16[3,3,64,16]{2,3,1,0:T(8,128)(2,1)}, u32[]{:S(2)}) copy-start(bf16[3,3,64,16]{2,3,1,0:T(8,128)(2,1)} %param.11) | copy-start | bytes 55300
  0.0 2.4 %copy-start.3 = (bf16[3,3,64,128]{3,2,1,0:T(8,128)(2,1)S(1)}, bf16[3,3,64,128]{3,2,1,0:T(8,128)(2,1)}, u32[]{:S(2)}) copy-start(bf16[3,3,64,128]{3,2,1,0:T(8,128)(2,1)} %km.1) | copy-start | bytes 442372
  1.0 1.4 %copy-start = (bf16[3,3,128,128]{3,2,1,0:T(8,128)(2,1)S(1)}, bf16[3,3,128,128]{3,2,1,0:T(8,128)(2,1)}, u32[]{:S(2)}) copy-start(bf16[3,3,128,128]{3,2,1,0:T(8,128)(2,1)} %kc.1) | copy-start | bytes 884740
  1.2 1.3 %copy-start.1 = (bf16[3,3,64,64]{3,2,1,0:T(8,128)(2,1)S(1)}, bf16[3,3,64,64]{3,2,1,0:T(8,128)(2,1)}, u32[]{:S(2)}) copy-start(bf16[3,3,64,64]{3,2,1,0:T(8,128)(2,1)} %k2.1) | copy-start | bytes 221188
  1.2 1.3 %copy-start.2 = (bf16[3,3,64,128]{3,2,1,0:T(8,128)(2,1)S(1)}, bf16[3,3,64,128]{3,2,1,0:T(8,128)(2,1)}, u32[]{:S(2)}) copy-start(bf16[3,3,64,128]{3,2,1,0:T(8,128)(2,1)} %ku.1) | copy-start | bytes 442372
  1.2 1.3 %copy-start.4 = (s32[2,32,128]{2,1,0:T(8,128)S(1)}, s32[2,32,128]{2,1,0:T(8,128)}, u32[]{:S(2)}) copy-start(s32[2,32,128]{2,1,0:T(8,128)} %tab_ref.1) | copy-start | bytes 98308
  1.2 1.2 %copy-start.5 = (bf16[8,64]{1,0:T(8,128)(2,1)S(1)}, bf16[8,64]{1,0:T(8,128)(2,1)}, u32[]{:S(2)}) copy-start(bf16[8,64]{1,0:T(8,128)(2,1)} %kp.1) | copy-start | bytes 3076
